TPU v7x, 32 devices: a whole 2x2x4 slice. The times are simulated.
32 devices in a mesh: group: 2 (over y), aper: 4 (over z), strip: 2 (over x), beam: 2 (over core).
Axes of the slice: x: 2, y: 2, z: 4, core: 2. Of those that a mesh axis runs over, the one named last changes fastest.
Arguments:
- partial_pictures: bfloat16 [2, 8, 128, 2048], P(None, ('group', 'aper'), 'beam', 'strip'), parts along dimension 1, may hold values from -6 to 6
- floor_input_direction: int32 [4, 8, 2, 128], P(None, ('group', 'aper'), None, 'beam'), parts along dimension 1, may hold values from 0 to 126
- higher_neighbour_blend: float32 [4, 8, 2, 128], P(None, ('group', 'aper'), None, 'beam'), parts along dimension 1, may hold values from 0 to 1
- integer_distance_bins: int32 [4, 8, 2, 128], P(None, ('group', 'aper'), None, 'beam'), parts along dimension 1, may hold values from -64 to 64
- distance_offset_fraction: float32 [4, 8, 2, 128], P(None, ('group', 'aper'), None, 'beam'), parts along dimension 1, may hold values from -0.5 to 0.5
- modulation_rotation: float32 [4, 8, 2, 128], P(None, ('group', 'aper'), None, 'beam'), parts along dimension 1, may hold values from -3.140625 to 3.140625
Outputs:
- focused: bfloat16 [2, 8, 128, 2048], P(None, ('group', 'aper'), 'beam', 'strip'), parts along dimension 1
There are 2 independent parts, one for each index of `group`. A program takes and returns all parts, laid end to end along the dimension named above; each array names one. Nothing has to cross between parts.
Inputs may be any that keep to these rules, and one draw needn't show every extreme that they name: `floor_input_direction`: a lower source beam below the last beam.
All inputs are finite; a program needn't handle non-finite values.
Results may differ from a plain program's by a relative error of at most 0.025.
Values may be sent and summed in bfloat16 or wider, within the bound.
A program may use at most 64 MiB of HBM per device.

v0:
```python
import functools
import math

import jax
import jax.numpy as jnp
import ml_dtypes
import numpy as np
from jax import lax
from jax.experimental import pallas as pl
from jax.experimental.pallas import tpu as pltpu
from jax.sharding import PartitionSpec as P

GUARD = 128
NUM_COMBINES = 4
CHUNK = 256
LANES = 128
MESH = pl.DeviceIdType.MESH
F32 = jnp.float32
BF16 = jnp.bfloat16


def transform_tables(strip_len):
    length = strip_len + 2 * GUARD
    half = length // 2
    sample = np.concatenate(
        [np.arange(GUARD, GUARD + strip_len), np.arange(GUARD), np.arange(GUARD + strip_len, length)]
    )
    freq = np.arange(half)
    angle = (sample[:, None] * freq[None, :] % length) * (2.0 * np.pi / length)
    cosines = np.cos(angle)
    sines = np.sin(angle)
    sines[:, 0] = 1.0 - 2.0 * (sample % 2)
    forward = np.concatenate([cosines, sines], axis=1).astype(ml_dtypes.bfloat16)
    inverse = forward[:strip_len].astype(np.float32).T.copy()
    inverse[0] *= 0.5
    inverse[half] *= 0.5
    return forward, inverse.astype(ml_dtypes.bfloat16)


def kernel(
    n_aper,
    n_strip,
    x_ref,
    floor_ref,
    blend_ref,
    bins_ref,
    part_ref,
    rot_ref,
    fwd_hbm,
    inv_hbm,
    out_ref,
    fwd,
    inv,
    full,
    guard,
    w_own,
    w_send,
    w_recv,
    s_main,
    s_guard,
    r_main,
    r_guard,
    x_own,
    acc,
    merged,
    cos_t,
    sin_t,
    table_sem,
    core_send,
    core_recv,
    edge_send,
    edge_recv,
    z_send,
    z_recv,
    w_send_sem,
    w_recv_sem,
):
    beams = x_ref.shape[1]
    all_beams = 2 * beams
    strip_len = x_ref.shape[2]
    chunks = strip_len // CHUNK
    length = strip_len + 2 * GUARD
    half = length // 2
    blocks = half // LANES
    bits = n_aper.bit_length() - 1
    order = [0, chunks - 1] + list(range(1, chunks - 1))

    aper = lax.axis_index("aper")
    strip = lax.axis_index("strip")
    beam = lax.axis_index("beam")
    other = 1 - beam
    has_left = strip > 0
    has_right = strip < n_strip - 1
    mine = pl.ds(pl.multiple_of(beam * beams, beams), beams)

    table_copies = [
        pltpu.make_async_copy(fwd_hbm, fwd, table_sem.at[0]),
        pltpu.make_async_copy(inv_hbm, inv, table_sem.at[1]),
    ]
    for copy in table_copies:
        copy.start()

    def flip(bit):
        return aper + bit - 2 * bit * ((aper // bit) % 2)

    def level_bit(level):
        bit = 1 << ((NUM_COMBINES - 1) % bits)
        for at in range(NUM_COMBINES - 1):
            bit = jnp.where(level == at, 1 << (at % bits), bit)
        return bit

    barrier = pltpu.get_barrier_semaphore()

    def greet(where):
        pl.semaphore_signal(barrier, inc=1, device_id=where, device_id_type=MESH)

    greet({"beam": other})
    partner_bits = sorted({1 << (at % bits) for at in range(NUM_COMBINES)})
    for bit in partner_bits:
        greet({"aper": flip(bit)})

    @pl.when(has_left)
    def _():
        greet({"strip": strip - 1})
        greet({"strip": strip - 1, "beam": other})

    @pl.when(has_right)
    def _():
        greet({"strip": strip + 1})
        greet({"strip": strip + 1, "beam": other})

    sides = has_left.astype(jnp.int32) + has_right.astype(jnp.int32)
    pl.semaphore_wait(barrier, 1 + len(partner_bits) + 2 * sides)

    def core_copy(level, j):
        place = full.at[level, j, :, mine, :]
        return pltpu.make_async_remote_copy(
            place, place, core_send.at[level, j], core_recv.at[level, j], {"beam": other}, MESH
        )

    def edge_copy(level, side, cross):
        j, at = (chunks - 1, CHUNK - GUARD) if side == 0 else (0, 0)
        target = strip + 1 if side == 0 else strip - 1
        return pltpu.make_async_remote_copy(
            full.at[level, j, :, mine, pl.ds(at, GUARD)],
            guard.at[level, side, :, mine, :],
            edge_send.at[level, side, cross],
            edge_recv.at[level, side, cross],
            {"strip": target, "beam": other if cross else beam},
            MESH,
        )

    def edge_wait(level, side, cross):
        place = guard.at[level, side, :, mine, :]
        pltpu.make_async_remote_copy(
            place, place, edge_send.at[level, side, cross], edge_recv.at[level, side, cross], {"beam": other}, MESH
        ).wait_recv()

    def z_copy(level, j):
        return pltpu.make_async_remote_copy(
            s_main.at[level, j],
            r_main.at[level, j],
            z_send.at[level, j],
            z_recv.at[level, j],
            {"aper": flip(level_bit(level))},
            MESH,
        )

    def z_guard_copy(level, side):
        return pltpu.make_async_remote_copy(
            s_guard.at[level, side],
            r_guard.at[level, side],
            z_send.at[level, chunks + side],
            z_recv.at[level, chunks + side],
            {"aper": flip(level_bit(level))},
            MESH,
        )

    def w_copy(level):
        return pltpu.make_async_remote_copy(
            w_send.at[level],
            w_recv.at[level],
            w_send_sem.at[level],
            w_recv_sem.at[level],
            {"aper": flip(level_bit(level))},
            MESH,
        )

    def distribute(level, j):
        core_copy(level, j).start()
        if j == 0:

            @pl.when(has_left)
            def _():
                for cross in range(2):
                    edge_copy(level, 1, cross).start()

        if j == chunks - 1:

            @pl.when(has_right)
            def _():
                for cross in range(2):
                    edge_copy(level, 0, cross).start()

    for j in order:
        full[0, j, :, mine, :] = x_ref[:, :, j * CHUNK : (j + 1) * CHUNK]
        distribute(0, j)

    eye = lax.broadcasted_iota(jnp.int32, (beams, beams), 0) == lax.broadcasted_iota(
        jnp.int32, (beams, beams), 1
    )

    def column(ref, level, slot):
        row = ref[level, slot : slot + 1, :].astype(F32)
        return jnp.sum(jnp.where(eye, jnp.broadcast_to(row, (beams, beams)), 0.0), axis=1, keepdims=True)

    def weights_of(level, slot):
        source = lax.broadcasted_iota(jnp.int32, (beams, all_beams), 1).astype(F32)
        chosen = column(floor_ref, level, slot)
        fraction = column(blend_ref, level, slot)
        return (
            jnp.where(source == chosen, 1.0 - fraction, 0.0)
            + jnp.where(source == chosen + 1.0, fraction, 0.0)
        ).astype(BF16)

    def send_weights(level, carry):
        w_send[level] = weights_of(level, 1)
        w_copy(level).start()
        return carry

    lax.fori_loop(0, NUM_COMBINES, send_weights, 0)

    @pl.when(jnp.logical_not(has_left))
    def _():
        guard[:, 0] = jnp.zeros((NUM_COMBINES,) + guard.shape[2:], BF16)
        r_guard[:, 0] = jnp.zeros((NUM_COMBINES,) + r_guard.shape[2:], BF16)

    @pl.when(jnp.logical_not(has_right))
    def _():
        guard[:, 1] = jnp.zeros((NUM_COMBINES,) + guard.shape[2:], BF16)
        r_guard[:, 1] = jnp.zeros((NUM_COMBINES,) + r_guard.shape[2:], BF16)

    def own_weights(level, carry):
        w_own[level] = weights_of(level, 0)
        return carry

    lax.fori_loop(0, NUM_COMBINES, own_weights, 0)

    step = 2.0 * math.pi / length
    lane = lax.broadcasted_iota(jnp.int32, (beams, LANES), 1)

    def level_body(level, carry):
        w_copy(level).wait_recv()
        weights = jnp.concatenate([w_recv[level], w_own[level]], axis=0)
        for j in order:
            core_copy(level, j).wait_recv()
            for c in range(2):
                mixed = jnp.dot(weights, full[level, j, c], preferred_element_type=F32).astype(BF16)
                s_main[level, j, c * beams : (c + 1) * beams, :] = mixed[:beams]
                x_own[c * beams : (c + 1) * beams, j * CHUNK : (j + 1) * CHUNK] = mixed[beams:]
            z_copy(level, j).start()
        for side, there in ((0, has_left), (1, has_right)):

            @pl.when(there)
            def _():
                for cross in range(2):
                    edge_wait(level, side, cross)

            at = strip_len + side * GUARD
            for c in range(2):
                mixed = jnp.dot(weights, guard[level, side, c], preferred_element_type=F32).astype(BF16)
                s_guard[level, side, c * beams : (c + 1) * beams, :] = mixed[:beams]
                x_own[c * beams : (c + 1) * beams, at : at + GUARD] = mixed[beams:]

            @pl.when(there)
            def _():
                z_guard_copy(level, side).start()

        turns = []
        for slot in range(2):
            sigma = column(bins_ref, level, slot) + column(part_ref, level, slot)
            rot = column(rot_ref, level, slot)
            base = lane.astype(F32) * (step * sigma)
            base_cos, base_sin = jnp.cos(base), jnp.sin(base)
            lead = lane.astype(F32) * (step * LANES * sigma)
            lead_cos, lead_sin = jnp.cos(lead), jnp.sin(lead)
            for a in range(blocks):
                a_cos, a_sin = lead_cos[:, a : a + 1], lead_sin[:, a : a + 1]
                cos_t[slot, :, a * LANES : (a + 1) * LANES] = base_cos * a_cos - base_sin * a_sin
                sin_t[slot, :, a * LANES : (a + 1) * LANES] = base_sin * a_cos + base_cos * a_sin
            nyquist = rot + jnp.where(lane == 0, math.pi * sigma, 0.0)
            scale = 2.0 / length
            first = (jnp.cos(nyquist) * scale, jnp.sin(nyquist) * scale)
            rest = (first[0][:, 1:2], first[1][:, 1:2])
            turns.append((rest, first))

        @pl.when(level == 0)
        def _():
            table_copies[0].wait()

        for at in range(0, length, CHUNK):
            acc[0, :, at : at + CHUNK] = jnp.dot(x_own[...], fwd[:, at : at + CHUNK], preferred_element_type=F32)
        for i, j in enumerate(order + [chunks]):
            if j < chunks:
                z_copy(level, j).wait_recv()
                piece = r_main[level, j]
            else:
                for side, there in ((0, has_left), (1, has_right)):

                    @pl.when(there)
                    def _():
                        z_guard_copy(level, side).wait_recv()

                piece = jnp.concatenate([r_guard[level, 0], r_guard[level, 1]], axis=1)
            for at in range(0, length, CHUNK):
                term = jnp.dot(piece, fwd[j * CHUNK : (j + 1) * CHUNK, at : at + CHUNK], preferred_element_type=F32)
                if i == 0:
                    acc[1, :, at : at + CHUNK] = term
                else:
                    acc[1, :, at : at + CHUNK] += term

        for a in range(blocks):
            low = slice(a * LANES, (a + 1) * LANES)
            high = slice(half + a * LANES, half + (a + 1) * LANES)
            total = [0.0, 0.0, 0.0, 0.0]
            for slot in range(2):
                p_re, p_im = acc[slot, :beams, low], acc[slot, beams:, low]
                q_re, q_im = acc[slot, :beams, high], acc[slot, beams:, high]
                c, s = cos_t[slot, :, low], sin_t[slot, :, low]
                (rc, rs), first = turns[slot]
                qc, qs = first if a == 0 else (rc, rs)
                u_re, u_im = p_re * c - q_re * s, p_im * c - q_im * s
                v_re, v_im = q_re * c + p_re * s, q_im * c + p_im * s
                total[0] += u_re * rc - u_im * rs
                total[1] += u_im * rc + u_re * rs
                total[2] += v_re * qc - v_im * qs
                total[3] += v_im * qc + v_re * qs
            merged[:beams, low] = total[0].astype(BF16)
            merged[beams:, low] = total[1].astype(BF16)
            merged[:beams, high] = total[2].astype(BF16)
            merged[beams:, high] = total[3].astype(BF16)

        @pl.when(level == 0)
        def _():
            table_copies[1].wait()

        for j in order:
            cols = slice(j * CHUNK, (j + 1) * CHUNK)
            result = jnp.dot(merged[...], inv[:, cols], preferred_element_type=F32).astype(BF16)

            @pl.when(level < NUM_COMBINES - 1)
            def _():
                full[level + 1, j, 0, mine, :] = result[:beams]
                full[level + 1, j, 1, mine, :] = result[beams:]
                distribute(level + 1, j)

            @pl.when(level == NUM_COMBINES - 1)
            def _():
                out_ref[0, :, cols] = result[:beams]
                out_ref[1, :, cols] = result[beams:]

        return carry

    lax.fori_loop(0, NUM_COMBINES, level_body, 0)

    def drain(level, carry):
        w_copy(level).wait_send()
        for j in range(chunks):
            core_copy(level, j).wait_send()
            z_copy(level, j).wait_send()

        @pl.when(has_right)
        def _():
            for cross in range(2):
                edge_copy(level, 0, cross).wait_send()
            z_guard_copy(level, 1).wait_send()

        @pl.when(has_left)
        def _():
            for cross in range(2):
                edge_copy(level, 1, cross).wait_send()
            z_guard_copy(level, 0).wait_send()

        return carry

    lax.fori_loop(0, NUM_COMBINES, drain, 0)


def shards(pictures, floors, blends, bins, parts, rots):
    current = pictures[:, 0]
    _, beams, strip_len = current.shape
    length = strip_len + 2 * GUARD
    half = length // 2
    chunks = strip_len // CHUNK
    rows = 2 * beams
    forward, inverse = transform_tables(strip_len)
    n = NUM_COMBINES
    vmem = pl.BlockSpec(memory_space=pltpu.VMEM)
    dma = pltpu.SemaphoreType.DMA
    out = pl.pallas_call(
        functools.partial(kernel, lax.axis_size("aper"), lax.axis_size("strip")),
        out_shape=jax.ShapeDtypeStruct(current.shape, BF16),
        in_specs=[vmem] * 6 + [pl.BlockSpec(memory_space=pl.ANY)] * 2,
        out_specs=vmem,
        scratch_shapes=[
            pltpu.VMEM((length, length), BF16),
            pltpu.VMEM((length, strip_len), BF16),
            pltpu.VMEM((n, chunks, 2, 2 * beams, CHUNK), BF16),
            pltpu.VMEM((n, 2, 2, 2 * beams, GUARD), BF16),
            pltpu.VMEM((n, beams, 2 * beams), BF16),
            pltpu.VMEM((n, beams, 2 * beams), BF16),
            pltpu.VMEM((n, beams, 2 * beams), BF16),
            pltpu.VMEM((n, chunks, rows, CHUNK), BF16),
            pltpu.VMEM((n, 2, rows, GUARD), BF16),
            pltpu.VMEM((n, chunks, rows, CHUNK), BF16),
            pltpu.VMEM((n, 2, rows, GUARD), BF16),
            pltpu.VMEM((rows, length), BF16),
            pltpu.VMEM((2, rows, length), F32),
            pltpu.VMEM((rows, length), BF16),
            pltpu.VMEM((2, beams, half), F32),
            pltpu.VMEM((2, beams, half), F32),
            dma((2,)),
            dma((n, chunks)),
            dma((n, chunks)),
            dma((n, 2, 2)),
            dma((n, 2, 2)),
            dma((n, chunks + 2)),
            dma((n, chunks + 2)),
            dma((n,)),
            dma((n,)),
        ],
        compiler_params=pltpu.CompilerParams(
            collective_id=0, has_side_effects=True, vmem_limit_bytes=56 * 1024 * 1024
        ),
    )(
        current,
        floors[:, 0],
        blends[:, 0],
        bins[:, 0],
        parts[:, 0],
        rots[:, 0],
        jnp.asarray(forward),
        jnp.asarray(inverse),
    )
    return out[:, None]


def solution(mesh):
    tables = P(None, ("group", "aper"), None, "beam")
    pictures = P(None, ("group", "aper"), "beam", "strip")
    return jax.shard_map(
        shards,
        mesh=mesh,
        in_specs=(pictures,) + (tables,) * 5,
        out_specs=pictures,
        check_vma=False,
    )
```

profile of v0, /device:TPU:0, one launch (start us, length us, event | category | flops | bytes accessed | tf_op | source)
XLA Modules:
  0.0 63.3 jit_solution(10239525420174270257)
XLA Ops:
  0.0 61.6 %shard_map.82 = bf16[2,64,1024]{2,1,0:T(8,128)(2,1)} custom-call(bf16[2,64,1024]{2,1,0:T(8,128)(2,1)} %bitcast.10, s32[4,2,64]{2,1,0:T(2,128)} %bitcast.11, f32[4,2,64]{2,1,0:T(2,128)} %bitcast.12, s32[4,2,64]{2,1,0:T(2,128)} %bitcast.13, f32[4,2,64]{2,1,0:T(2,128)} %bitcast.14, f32[4,2,64]{2,1,0:T(2,128)} %bitcast.15, ...), custom_call_target="tpu_custom_call" | custom-call | tf_op jit(solution)/shard_map/pallas_call | solution.py:400
  61.6 1.7 %copy.11 = bf16[2,1,64,1024]{3,2,1,0:T(8,128)(2,1)} copy(bf16[2,1,64,1024]{3,2,1,0:T(8,128)(2,1)} %bitcast.9) | data formatting | bytes 524288
where the time goes:
time: 63.4 us; the launch traced here: 63.3 us
  Pallas kernels  61.6 us (97%)
  local copies, waits for them, and re-layouts  1.67 us (3%)
    pallas_call x1, Pallas kernels, shards(): pl.pallas_call(functools.partial(kernel, lax.axis_size('aper'), lax.axis_...  61.6 us
    unnamed x1, local copies, waits for them, and re-layouts  1.67 us

commit v1 on v0

--- a/solution.py
+++ b/solution.py
@@ -52,12 +52,10 @@
     fwd,
     inv,
     full,
-    guard,
     w_own,
     w_send,
     w_recv,
     s_main,
-    s_guard,
     r_main,
     r_guard,
     x_own,
@@ -122,15 +120,13 @@
     @pl.when(has_left)
     def _():
         greet({"strip": strip - 1})
-        greet({"strip": strip - 1, "beam": other})
 
     @pl.when(has_right)
     def _():
         greet({"strip": strip + 1})
-        greet({"strip": strip + 1, "beam": other})
 
     sides = has_left.astype(jnp.int32) + has_right.astype(jnp.int32)
-    pl.semaphore_wait(barrier, 1 + len(partner_bits) + 2 * sides)
+    pl.semaphore_wait(barrier, 1 + len(partner_bits) + sides)
 
     def core_copy(level, j):
         place = full.at[level, j, :, mine, :]
@@ -138,23 +134,44 @@
             place, place, core_send.at[level, j], core_recv.at[level, j], {"beam": other}, MESH
         )
 
-    def edge_copy(level, side, cross):
-        j, at = (chunks - 1, CHUNK - GUARD) if side == 0 else (0, 0)
-        target = strip + 1 if side == 0 else strip - 1
+    def edge_copy(level, slot, side, outward=True):
+        target = strip + 1 if (side == 0) == outward else strip - 1
+        if slot == 0:
+            at = strip_len - GUARD if side == 0 else 0
+            source = x_own.at[level, :, pl.ds(at, GUARD)]
+            place = x_own.at[level, :, pl.ds(strip_len + side * GUARD, GUARD)]
+        else:
+            j, at = (chunks - 1, CHUNK - GUARD) if side == 0 else (0, 0)
+            source = r_main.at[level, j, :, pl.ds(at, GUARD)]
+            place = r_guard.at[level, :, pl.ds(side * GUARD, GUARD)]
         return pltpu.make_async_remote_copy(
-            full.at[level, j, :, mine, pl.ds(at, GUARD)],
-            guard.at[level, side, :, mine, :],
-            edge_send.at[level, side, cross],
-            edge_recv.at[level, side, cross],
-            {"strip": target, "beam": other if cross else beam},
+            source,
+            place,
+            edge_send.at[level, slot, side],
+            edge_recv.at[level, slot, side],
+            {"strip": target},
             MESH,
         )
 
-    def edge_wait(level, side, cross):
-        place = guard.at[level, side, :, mine, :]
-        pltpu.make_async_remote_copy(
-            place, place, edge_send.at[level, side, cross], edge_recv.at[level, side, cross], {"beam": other}, MESH
-        ).wait_recv()
+    def send_edges(level, slot, j):
+        if j == 0:
+
+            @pl.when(has_left)
+            def _():
+                edge_copy(level, slot, 1).start()
+
+        if j == chunks - 1:
+
+            @pl.when(has_right)
+            def _():
+                edge_copy(level, slot, 0).start()
+
+    def await_edges(level, slot):
+        for side, there in ((0, has_left), (1, has_right)):
+
+            @pl.when(there)
+            def _():
+                edge_copy(level, slot, side, outward=False).wait_recv()
 
     def z_copy(level, j):
         return pltpu.make_async_remote_copy(
@@ -166,16 +183,6 @@
             MESH,
         )
 
-    def z_guard_copy(level, side):
-        return pltpu.make_async_remote_copy(
-            s_guard.at[level, side],
-            r_guard.at[level, side],
-            z_send.at[level, chunks + side],
-            z_recv.at[level, chunks + side],
-            {"aper": flip(level_bit(level))},
-            MESH,
-        )
-
     def w_copy(level):
         return pltpu.make_async_remote_copy(
             w_send.at[level],
@@ -188,19 +195,6 @@
 
     def distribute(level, j):
         core_copy(level, j).start()
-        if j == 0:
-
-            @pl.when(has_left)
-            def _():
-                for cross in range(2):
-                    edge_copy(level, 1, cross).start()
-
-        if j == chunks - 1:
-
-            @pl.when(has_right)
-            def _():
-                for cross in range(2):
-                    edge_copy(level, 0, cross).start()
 
     for j in order:
         full[0, j, :, mine, :] = x_ref[:, :, j * CHUNK : (j + 1) * CHUNK]
@@ -232,13 +226,15 @@
 
     @pl.when(jnp.logical_not(has_left))
     def _():
-        guard[:, 0] = jnp.zeros((NUM_COMBINES,) + guard.shape[2:], BF16)
-        r_guard[:, 0] = jnp.zeros((NUM_COMBINES,) + r_guard.shape[2:], BF16)
+        none = jnp.zeros((NUM_COMBINES, 2 * beams, GUARD), BF16)
+        x_own[:, :, strip_len + 0 * GUARD : strip_len + 1 * GUARD] = none
+        r_guard[:, :, 0 * GUARD : 1 * GUARD] = none
 
     @pl.when(jnp.logical_not(has_right))
     def _():
-        guard[:, 1] = jnp.zeros((NUM_COMBINES,) + guard.shape[2:], BF16)
-        r_guard[:, 1] = jnp.zeros((NUM_COMBINES,) + r_guard.shape[2:], BF16)
+        none = jnp.zeros((NUM_COMBINES, 2 * beams, GUARD), BF16)
+        x_own[:, :, strip_len + 1 * GUARD : strip_len + 2 * GUARD] = none
+        r_guard[:, :, 1 * GUARD : 2 * GUARD] = none
 
     def own_weights(level, carry):
         w_own[level] = weights_of(level, 0)
@@ -257,25 +253,9 @@
             for c in range(2):
                 mixed = jnp.dot(weights, full[level, j, c], preferred_element_type=F32).astype(BF16)
                 s_main[level, j, c * beams : (c + 1) * beams, :] = mixed[:beams]
-                x_own[c * beams : (c + 1) * beams, j * CHUNK : (j + 1) * CHUNK] = mixed[beams:]
+                x_own[level, c * beams : (c + 1) * beams, j * CHUNK : (j + 1) * CHUNK] = mixed[beams:]
             z_copy(level, j).start()
-        for side, there in ((0, has_left), (1, has_right)):
-
-            @pl.when(there)
-            def _():
-                for cross in range(2):
-                    edge_wait(level, side, cross)
-
-            at = strip_len + side * GUARD
-            for c in range(2):
-                mixed = jnp.dot(weights, guard[level, side, c], preferred_element_type=F32).astype(BF16)
-                s_guard[level, side, c * beams : (c + 1) * beams, :] = mixed[:beams]
-                x_own[c * beams : (c + 1) * beams, at : at + GUARD] = mixed[beams:]
-
-            @pl.when(there)
-            def _():
-                z_guard_copy(level, side).start()
-
+            send_edges(level, 0, j)
         turns = []
         for slot in range(2):
             sigma = column(bins_ref, level, slot) + column(part_ref, level, slot)
@@ -298,20 +278,17 @@
         def _():
             table_copies[0].wait()
 
+        await_edges(level, 0)
         for at in range(0, length, CHUNK):
-            acc[0, :, at : at + CHUNK] = jnp.dot(x_own[...], fwd[:, at : at + CHUNK], preferred_element_type=F32)
-        for i, j in enumerate(order + [chunks]):
+            acc[0, :, at : at + CHUNK] = jnp.dot(x_own[level], fwd[:, at : at + CHUNK], preferred_element_type=F32)
+        for i, j in enumerate(order[:-1] + [chunks, order[-1]]):
             if j < chunks:
                 z_copy(level, j).wait_recv()
+                send_edges(level, 1, j)
                 piece = r_main[level, j]
             else:
-                for side, there in ((0, has_left), (1, has_right)):
-
-                    @pl.when(there)
-                    def _():
-                        z_guard_copy(level, side).wait_recv()
-
-                piece = jnp.concatenate([r_guard[level, 0], r_guard[level, 1]], axis=1)
+                await_edges(level, 1)
+                piece = r_guard[level]
             for at in range(0, length, CHUNK):
                 term = jnp.dot(piece, fwd[j * CHUNK : (j + 1) * CHUNK, at : at + CHUNK], preferred_element_type=F32)
                 if i == 0:
@@ -369,17 +346,15 @@
             core_copy(level, j).wait_send()
             z_copy(level, j).wait_send()
 
-        @pl.when(has_right)
-        def _():
-            for cross in range(2):
-                edge_copy(level, 0, cross).wait_send()
-            z_guard_copy(level, 1).wait_send()
-
-        @pl.when(has_left)
-        def _():
-            for cross in range(2):
-                edge_copy(level, 1, cross).wait_send()
-            z_guard_copy(level, 0).wait_send()
+        for slot in range(2):
+
+            @pl.when(has_right)
+            def _():
+                edge_copy(level, slot, 0).wait_send()
+
+            @pl.when(has_left)
+            def _():
+                edge_copy(level, slot, 1).wait_send()
 
         return carry
 
@@ -406,15 +381,13 @@
             pltpu.VMEM((length, length), BF16),
             pltpu.VMEM((length, strip_len), BF16),
             pltpu.VMEM((n, chunks, 2, 2 * beams, CHUNK), BF16),
-            pltpu.VMEM((n, 2, 2, 2 * beams, GUARD), BF16),
             pltpu.VMEM((n, beams, 2 * beams), BF16),
             pltpu.VMEM((n, beams, 2 * beams), BF16),
             pltpu.VMEM((n, beams, 2 * beams), BF16),
             pltpu.VMEM((n, chunks, rows, CHUNK), BF16),
-            pltpu.VMEM((n, 2, rows, GUARD), BF16),
             pltpu.VMEM((n, chunks, rows, CHUNK), BF16),
-            pltpu.VMEM((n, 2, rows, GUARD), BF16),
-            pltpu.VMEM((rows, length), BF16),
+            pltpu.VMEM((n, rows, 2 * GUARD), BF16),
+            pltpu.VMEM((n, rows, length), BF16),
             pltpu.VMEM((2, rows, length), F32),
             pltpu.VMEM((rows, length), BF16),
             pltpu.VMEM((2, beams, half), F32),
@@ -424,8 +397,8 @@
             dma((n, chunks)),
             dma((n, 2, 2)),
             dma((n, 2, 2)),
-            dma((n, chunks + 2)),
-            dma((n, chunks + 2)),
+            dma((n, chunks)),
+            dma((n, chunks)),
             dma((n,)),
             dma((n,)),
         ],

time: 63.4 us -> 62.6 us (0.987)
  Pallas kernels: 61.6 us -> 60.8 us
    pallas_call x1, Pallas kernels: 61.6 us -> 60.8 us  [shards(): pl.pallas_call(functools.partial(kernel, lax.axis_size('aper'), lax.axis_...]
where the time goes in v1:
time: 62.6 us; the launch traced here: 62.4 us
  Pallas kernels  60.8 us (97%)
  local copies, waits for them, and re-layouts  1.67 us (3%)
    pallas_call x1, Pallas kernels, shards(): pl.pallas_call(functools.partial(kernel, lax.axis_size('aper'), lax.axis_...  60.8 us
    unnamed x1, local copies, waits for them, and re-layouts  1.67 us

profile of v1, /device:TPU:0, one launch (start us, length us, event | category | flops | bytes accessed | tf_op | source)
XLA Modules:
  0.0 62.4 jit_solution(9483485135200412766)
XLA Ops:
  0.0 60.8 %shard_map.82 = bf16[2,64,1024]{2,1,0:T(8,128)(2,1)} custom-call(bf16[2,64,1024]{2,1,0:T(8,128)(2,1)} %bitcast.10, s32[4,2,64]{2,1,0:T(2,128)} %bitcast.11, f32[4,2,64]{2,1,0:T(2,128)} %bitcast.12, s32[4,2,64]{2,1,0:T(2,128)} %bitcast.13, f32[4,2,64]{2,1,0:T(2,128)} %bitcast.14, f32[4,2,64]{2,1,0:T(2,128)} %bitcast.15, ...), custom_call_target="tpu_custom_call" | custom-call | tf_op jit(solution)/shard_map/pallas_call | solution.py:375
  60.8 1.7 %copy.11 = bf16[2,1,64,1024]{3,2,1,0:T(8,128)(2,1)} copy(bf16[2,1,64,1024]{3,2,1,0:T(8,128)(2,1)} %bitcast.9) | data formatting | bytes 524288

commit v2 on v1

--- a/solution.py
+++ b/solution.py
@@ -278,10 +278,11 @@
         def _():
             table_copies[0].wait()
 
-        await_edges(level, 0)
         for at in range(0, length, CHUNK):
-            acc[0, :, at : at + CHUNK] = jnp.dot(x_own[level], fwd[:, at : at + CHUNK], preferred_element_type=F32)
-        for i, j in enumerate(order[:-1] + [chunks, order[-1]]):
+            acc[0, :, at : at + CHUNK] = jnp.dot(
+                x_own[level, :, :strip_len], fwd[:strip_len, at : at + CHUNK], preferred_element_type=F32
+            )
+        for i, j in enumerate(order + [chunks]):
             if j < chunks:
                 z_copy(level, j).wait_recv()
                 send_edges(level, 1, j)
@@ -289,6 +290,13 @@
             else:
                 await_edges(level, 1)
                 piece = r_guard[level]
+            if i == chunks - 1:
+                await_edges(level, 0)
+                own = x_own[level, :, strip_len:]
+                for at in range(0, length, CHUNK):
+                    acc[0, :, at : at + CHUNK] += jnp.dot(
+                        own, fwd[strip_len:, at : at + CHUNK], preferred_element_type=F32
+                    )
             for at in range(0, length, CHUNK):
                 term = jnp.dot(piece, fwd[j * CHUNK : (j + 1) * CHUNK, at : at + CHUNK], preferred_element_type=F32)
                 if i == 0:

time: 62.6 us -> 61.6 us (0.984)
  Pallas kernels: 60.8 us -> 59.7 us
    pallas_call x1, Pallas kernels: 60.8 us -> 59.7 us  [shards(): pl.pallas_call(functools.partial(kernel, lax.axis_size('aper'), lax.axis_...]
where the time goes in v2:
time: 61.6 us; the launch traced here: 61.4 us
  Pallas kernels  59.7 us (97%)
  local copies, waits for them, and re-layouts  1.67 us (3%)
    pallas_call x1, Pallas kernels, shards(): pl.pallas_call(functools.partial(kernel, lax.axis_size('aper'), lax.axis_...  59.7 us
    unnamed x1, local copies, waits for them, and re-layouts  1.67 us

profile of v2, /device:TPU:0, one launch (start us, length us, event | category | flops | bytes accessed | tf_op | source)
XLA Modules:
  0.0 61.4 jit_solution(17190840409835096182)
XLA Ops:
  0.0 59.7 %shard_map.82 = bf16[2,64,1024]{2,1,0:T(8,128)(2,1)} custom-call(bf16[2,64,1024]{2,1,0:T(8,128)(2,1)} %bitcast.10, s32[4,2,64]{2,1,0:T(2,128)} %bitcast.11, f32[4,2,64]{2,1,0:T(2,128)} %bitcast.12, s32[4,2,64]{2,1,0:T(2,128)} %bitcast.13, f32[4,2,64]{2,1,0:T(2,128)} %bitcast.14, f32[4,2,64]{2,1,0:T(2,128)} %bitcast.15, ...), custom_call_target="tpu_custom_call" | custom-call | tf_op jit(solution)/shard_map/pallas_call | solution.py:383
  59.7 1.7 %copy.11 = bf16[2,1,64,1024]{3,2,1,0:T(8,128)(2,1)} copy(bf16[2,1,64,1024]{3,2,1,0:T(8,128)(2,1)} %bitcast.9) | data formatting | bytes 524288
